TPU v7x, 32 devices: a whole 2x2x4 slice. The times are simulated.
32 devices in a mesh: row: 4 (over x, core), col: 4 (over z), layer: 2 (over y).
Axes of the slice: x: 2, y: 2, z: 4, core: 2. Of those that a mesh axis runs over, the one named last changes fastest.
Arguments:
- a_values: float32 [32, 4, 2, 1, 64, 384], P('row', 'col', 'layer'), may hold values from -0.3125 to 0.3125
- a_columns: int32 [32, 4, 2, 1, 6], P('row', 'col', 'layer'), may hold values from 0 to 15
- b_values: float32 [64, 4, 2, 64, 512], P('row', 'col', 'layer'), may hold values from -6 to 6
- b_columns: int32 [64, 4, 2, 8], P('row', 'col', 'layer'), may hold values from 0 to 31
- keep_columns: int32 [32, 4, 4], P('row', 'col'), may hold values from 0 to 31
Outputs:
- kept_blocks: float32 [32, 4, 64, 256], P(('row', 'layer'), 'col')
All inputs are finite; a program needn't handle non-finite values.
Results may differ from a plain program's by a relative error of at most 0.0003.
Values sent between devices are 32-bit elements; how exact they have to be, the bound alone decides.
A program may use at most 64 MiB of HBM per device.

v0:
```python
import jax
import jax.numpy as jnp
from jax import lax
from jax.sharding import PartitionSpec as P

BLK = 64
SLOTS_A = 6
SLOTS_B = 8
KEEP = 4


def shifted(x, axis, by):
    size = lax.axis_size(axis)
    return lax.ppermute(x, axis, [(i, (i + by) % size) for i in range(size)])


def block_term(left_values, left_index, right_values, right_index, keep_list):
    row_count = left_values.shape[0]
    blocks = left_values.reshape(row_count, BLK, SLOTS_A, BLK)
    gathered = jnp.take(right_values, left_index, axis=0)
    products = jnp.einsum("iawb,iwbv->iwav", blocks, gathered, precision=lax.Precision.HIGHEST)
    targets = jnp.take(right_index, left_index, axis=0)
    matches = (targets[:, :, :, None] == keep_list[:, None, None, :]).astype(jnp.float32)
    products = products.reshape(row_count, SLOTS_A, BLK, SLOTS_B, BLK)
    result = jnp.einsum("iwvu,iwavc->iauc", matches, products, precision=lax.Precision.HIGHEST)
    return result.reshape(row_count, BLK, KEEP * BLK)


def panel_term(left_values, left_index, right_values, right_index, keep_list):
    row_count = left_values.shape[0]
    groups = row_count // 4

    def group_term(pieces):
        return block_term(pieces[0], pieces[1], right_values, right_index, pieces[2])

    grouped = lax.map(
        group_term,
        (
            left_values.reshape(groups, 4, BLK, SLOTS_A * BLK),
            left_index.reshape(groups, 4, SLOTS_A),
            keep_list.reshape(groups, 4, KEEP),
        ),
    )
    return grouped.reshape(row_count, BLK, KEEP * BLK)


def per_device(a_values, a_columns, b_values, b_columns, keep_columns):
    grid_rows = lax.axis_size("row")
    grid_cols = lax.axis_size("col")
    row_place = lax.axis_index("row")
    col_place = lax.axis_index("col")
    all_values = a_values[:, 0, 0]
    all_index = a_columns[:, 0, 0]
    own_image = (row_place + col_place) % grid_rows // grid_cols
    receiver_col = (col_place + grid_cols - 1) % grid_cols
    sent_image = (row_place + receiver_col + 1) % grid_rows // grid_cols
    left_values = lax.dynamic_index_in_dim(all_values, own_image, 1, keepdims=False)
    left_index = lax.dynamic_index_in_dim(all_index, own_image, 1, keepdims=False)
    send_values = lax.dynamic_index_in_dim(all_values, sent_image, 1, keepdims=False)
    send_index = lax.dynamic_index_in_dim(all_index, sent_image, 1, keepdims=False)
    right_values = b_values[:, 0, 0]
    right_index = b_columns[:, 0, 0]
    keep_list = keep_columns[:, 0]
    moved_values, moved_index = shifted((send_values, send_index), "col", -1)
    first_term = panel_term(left_values, left_index, right_values, right_index, keep_list)
    next_values, next_index = shifted((right_values, right_index), "row", -1)
    running = first_term + panel_term(moved_values, moved_index, next_values, next_index, keep_list)
    summed = lax.psum_scatter(running, "layer", scatter_dimension=0, tiled=True)
    return summed[:, None]


def solution(mesh):
    placed = (
        P("row", "col", "layer", None, None, None),
        P("row", "col", "layer", None, None),
        P("row", "col", "layer", None, None),
        P("row", "col", "layer", None),
        P("row", "col", None),
    )
    return jax.shard_map(
        per_device,
        mesh=mesh,
        in_specs=placed,
        out_specs=P(("row", "layer"), "col", None, None),
        check_vma=False,
    )
```

profile of v0, /device:TPU:0, one launch (start us, length us, event | category | flops | bytes accessed | tf_op | source)
XLA Modules:
  0.0 138.6 jit_solution(15121122950348518226)
XLA Ops:
  6.5 2.4 %collective-permute-start.2 = (f32[16,64,512]{2,1,0:T(8,128)}, f32[16,64,512]{2,1,0:T(8,128)}, u32[]{:S(2)}, u32[]{:S(2)}) collective-permute-start(f32[16,64,512]{2,1,0:T(8,128)} %bitcast.87), channel_id=1, source_target_pairs={{0,24},{8,0},{16,8},{24,16},{1,25},{9,1},{17,9},{25,17},{2,26},{10... | collective-permute-start | bytes 6291464 | tf_op jit(solution)/shard_map/ppermute | solution.py:14
  8.9 0.7 collective-permute-start.3
  9.6 1.3 copy.22
  10.9 3.6 %collective-permute-start.1 = (s32[8,6]{1,0:T(8,128)}, s32[8,6]{1,0:T(8,128)}, u32[]{:S(2)}, u32[]{:S(2)}) collective-permute-start(s32[8,6]{1,0:T(8,128)} %bitcast.22), channel_id=1, source_target_pairs={{0,6},{2,0},{4,2},{6,4},{1,7},{3,1},{5,3},{7,5},{8,14},{10,8},{12,... | collective-permute-start | bytes 584 | tf_op jit(solution)/shard_map/ppermute | solution.py:14
  15.0 0.8 copy.23
  15.8 0.8 copy.32
  16.5 0.9 broadcast.33.clone
  17.4 48.8 %while.20 = (s32[]{:T(128)}, f32[2,4,64,256]{3,2,1,0:T(8,128)}, f32[2,4,64,384]{3,2,1,0:T(8,128)}, s32[2,4,6]{2,1,0:T(4,128)}, f32[16,64,512]{2,1,0:T(8,128)}, /...) while((s32[]{:T(128)}, f32[2,4,64,256]{3,2,1,0:T(8,128)}, f32[2,4,64,384]{3,2,1,0:T(8,128)}, ...), condition=%wide.region_1.4_spmd, body=%wide.region_0.3_spmd.sunk | while | flops 642517056 | bytes 29504960 | solution.py:36
  17.4 1.2 compare_and_fusion.4
  18.7 2.3 %gather_fusion = f32[24,64,512]{2,1,0:T(8,128)S(1)} fusion(f32[16,64,512]{2,1,0:T(8,128)} %get-tuple-element.257, s32[1024]{0:T(1024)S(1)} %pad_clamp_fusion.4), kind=kCustom, calls=%fused_computation.clone.clone.1 | custom fusion | bytes 6291552 | tf_op jit(solution)/shard_map/while/body/eval_jaxpr/jit(_take)/gather | solution.py:20
  21.0 1.0 constant_dynamic-slice_fusion.4
  22.1 1.2 reshape.140
  23.3 5.8 %fusion.36 = f32[4,6,64,512]{3,2,1,0:T(8,128)} fusion(f32[4,6,64,512]{3,2,1,0:T(8,128)S(1)} %bitcast.85, pred[4,6]{1,0:T(4,128)(4,1)} %get-tuple-element.227, f32[4,64,6,64]{3,2,1,0:T(8,128)} %reshape.140), kind=kOutput, calls=%fused_computation.4.clone.1 | convolution fusion | flops 604766208 | bytes 6684696 | tf_op jit(solution)/shard_map/while/body/eval_jaxpr/iawb,iwbv->iwav/dot_general | solution.py:21
  29.1 5.6 %reshape.141 = f32[4,6,64,8,64]{4,3,2,1,0:T(8,128)} reshape(f32[4,6,64,512]{3,2,1,0:T(8,128)} %fusion.36) | data formatting | bytes 6291456 | tf_op jit(solution)/shard_map/while/body/eval_jaxpr/reshape | solution.py:24
  34.7 0.6 gather_fusion.1
  35.6 5.0 %convolution_bitcast_fusion.4 = f32[4,64,4,64]{3,2,1,0:T(4,128)S(1)} fusion(f32[4,6,64,8,64]{4,3,2,1,0:T(8,128)} %reshape.141, s32[4,4]{1,0:T(4,128)S(1)} %dynamic-slice_bitcast_fusion.4, s32[4,6,8]{2,1,0:T(8,128)S(1)} %copy.45), kind=kOutput, calls=%fused_computation.8.clone.1 | convolution fusion | flops 37749504 | bytes 3408704 | tf_op jit(solution)/shard_map/while/body/eval_jaxpr/iwvu,iwavc->iauc/dot_general | solution.py:25
  41.0 0.8 copy-done.3
  41.8 1.2 compare_and_fusion.4
  43.1 2.3 %gather_fusion = f32[24,64,512]{2,1,0:T(8,128)S(1)} fusion(f32[16,64,512]{2,1,0:T(8,128)} %get-tuple-element.257, s32[1024]{0:T(1024)S(1)} %pad_clamp_fusion.4), kind=kCustom, calls=%fused_computation.clone.clone.1 | custom fusion | bytes 6291552 | tf_op jit(solution)/shard_map/while/body/eval_jaxpr/jit(_take)/gather | solution.py:20
  45.5 1.0 constant_dynamic-slice_fusion.4
  46.5 1.2 reshape.140
  47.7 5.8 %fusion.36 = f32[4,6,64,512]{3,2,1,0:T(8,128)} fusion(f32[4,6,64,512]{3,2,1,0:T(8,128)S(1)} %bitcast.85, pred[4,6]{1,0:T(4,128)(4,1)} %get-tuple-element.227, f32[4,64,6,64]{3,2,1,0:T(8,128)} %reshape.140), kind=kOutput, calls=%fused_computation.4.clone.1 | convolution fusion | flops 604766208 | bytes 6684696 | tf_op jit(solution)/shard_map/while/body/eval_jaxpr/iawb,iwbv->iwav/dot_general | solution.py:21
  53.5 5.6 %reshape.141 = f32[4,6,64,8,64]{4,3,2,1,0:T(8,128)} reshape(f32[4,6,64,512]{3,2,1,0:T(8,128)} %fusion.36) | data formatting | bytes 6291456 | tf_op jit(solution)/shard_map/while/body/eval_jaxpr/reshape | solution.py:24
  60.0 5.0 %convolution_bitcast_fusion.4 = f32[4,64,4,64]{3,2,1,0:T(4,128)S(1)} fusion(f32[4,6,64,8,64]{4,3,2,1,0:T(8,128)} %reshape.141, s32[4,4]{1,0:T(4,128)S(1)} %dynamic-slice_bitcast_fusion.4, s32[4,6,8]{2,1,0:T(8,128)S(1)} %copy.45), kind=kOutput, calls=%fused_computation.8.clone.1 | convolution fusion | flops 37749504 | bytes 3408704 | tf_op jit(solution)/shard_map/while/body/eval_jaxpr/iwvu,iwavc->iauc/dot_general | solution.py:25
  65.4 0.8 copy-done.3
  66.2 0.8 copy.26
  66.9 0.9 broadcast.33.clone.1
  67.9 48.8 %while.21 = (s32[]{:T(128)}, f32[2,4,64,256]{3,2,1,0:T(8,128)}, f32[2,4,64,384]{3,2,1,0:T(8,128)}, s32[2,4,6]{2,1,0:T(4,128)}, f32[16,64,512]{2,1,0:T(8,128)}, /...) while((s32[]{:T(128)}, f32[2,4,64,256]{3,2,1,0:T(8,128)}, f32[2,4,64,384]{3,2,1,0:T(8,128)}, ...), condition=%wide.region_3.6_spmd, body=%wide.region_2.5_spmd.sunk | while | flops 642517056 | bytes 29504960 | solution.py:36
  67.9 1.1 compare_and_fusion.5
  69.1 2.3 %gather_fusion.2 = f32[24,64,512]{2,1,0:T(8,128)S(1)} fusion(f32[16,64,512]{2,1,0:T(8,128)} %get-tuple-element.281, s32[1024]{0:T(1024)S(1)} %pad_clamp_fusion.5), kind=kCustom, calls=%fused_computation.2.clone.clone.1 | custom fusion | bytes 6291552 | tf_op jit(solution)/shard_map/while/body/eval_jaxpr/jit(_take)/gather | solution.py:20
  71.4 1.0 constant_dynamic-slice_fusion.5
  72.5 1.2 reshape.148
  73.7 5.8 %fusion.41 = f32[4,6,64,512]{3,2,1,0:T(8,128)} fusion(f32[4,6,64,512]{3,2,1,0:T(8,128)S(1)} %bitcast.86, pred[4,6]{1,0:T(4,128)(4,1)} %get-tuple-element.236, f32[4,64,6,64]{3,2,1,0:T(8,128)} %reshape.148), kind=kOutput, calls=%fused_computation.22.clone.1 | convolution fusion | flops 604766208 | bytes 6684696 | tf_op jit(solution)/shard_map/while/body/eval_jaxpr/iawb,iwbv->iwav/dot_general | solution.py:21
  79.5 5.6 %reshape.149 = f32[4,6,64,8,64]{4,3,2,1,0:T(8,128)} reshape(f32[4,6,64,512]{3,2,1,0:T(8,128)} %fusion.41) | data formatting | bytes 6291456 | tf_op jit(solution)/shard_map/while/body/eval_jaxpr/reshape | solution.py:24
  85.1 0.6 gather_fusion.3
  86.0 5.0 %convolution_bitcast_fusion.5 = f32[4,64,4,64]{3,2,1,0:T(4,128)S(1)} fusion(f32[4,6,64,8,64]{4,3,2,1,0:T(8,128)} %reshape.149, s32[4,4]{1,0:T(4,128)S(1)} %dynamic-slice_bitcast_fusion.5, s32[4,6,8]{2,1,0:T(8,128)S(1)} %copy.48), kind=kOutput, calls=%fused_computation.26.clone.1 | convolution fusion | flops 37749504 | bytes 3408704 | tf_op jit(solution)/shard_map/while/body/eval_jaxpr/iwvu,iwavc->iauc/dot_general | solution.py:25
  91.4 0.9 copy-done.1
  92.2 1.2 compare_and_fusion.5
  93.5 2.3 %gather_fusion.2 = f32[24,64,512]{2,1,0:T(8,128)S(1)} fusion(f32[16,64,512]{2,1,0:T(8,128)} %get-tuple-element.281, s32[1024]{0:T(1024)S(1)} %pad_clamp_fusion.5), kind=kCustom, calls=%fused_computation.2.clone.clone.1 | custom fusion | bytes 6291552 | tf_op jit(solution)/shard_map/while/body/eval_jaxpr/jit(_take)/gather | solution.py:20
  95.9 1.0 constant_dynamic-slice_fusion.5
  96.9 1.2 reshape.148
  98.1 5.8 %fusion.41 = f32[4,6,64,512]{3,2,1,0:T(8,128)} fusion(f32[4,6,64,512]{3,2,1,0:T(8,128)S(1)} %bitcast.86, pred[4,6]{1,0:T(4,128)(4,1)} %get-tuple-element.236, f32[4,64,6,64]{3,2,1,0:T(8,128)} %reshape.148), kind=kOutput, calls=%fused_computation.22.clone.1 | convolution fusion | flops 604766208 | bytes 6684696 | tf_op jit(solution)/shard_map/while/body/eval_jaxpr/iawb,iwbv->iwav/dot_general | solution.py:21
  103.9 5.6 %reshape.149 = f32[4,6,64,8,64]{4,3,2,1,0:T(8,128)} reshape(f32[4,6,64,512]{3,2,1,0:T(8,128)} %fusion.41) | data formatting | bytes 6291456 | tf_op jit(solution)/shard_map/while/body/eval_jaxpr/reshape | solution.py:24
  109.5 0.6 gather_fusion.3
  110.4 5.0 %convolution_bitcast_fusion.5 = f32[4,64,4,64]{3,2,1,0:T(4,128)S(1)} fusion(f32[4,6,64,8,64]{4,3,2,1,0:T(8,128)} %reshape.149, s32[4,4]{1,0:T(4,128)S(1)} %dynamic-slice_bitcast_fusion.5, s32[4,6,8]{2,1,0:T(8,128)S(1)} %copy.48), kind=kOutput, calls=%fused_computation.26.clone.1 | convolution fusion | flops 37749504 | bytes 3408704 | tf_op jit(solution)/shard_map/while/body/eval_jaxpr/iwvu,iwavc->iauc/dot_general | solution.py:25
  115.8 0.9 copy-done.1
  116.6 2.1 %add.37 = f32[2,4,64,256]{3,2,1,0:T(8,128)} add(f32[2,4,64,256]{3,2,1,0:T(8,128)} %get-tuple-element.81, f32[2,4,64,256]{3,2,1,0:T(8,128)} %get-tuple-element.82) | non-fusion elementwise | flops 131072 | bytes 1572864 | tf_op jit(solution)/shard_map/add | solution.py:67
  118.7 13.0 %reduce-scatter.2.cloned.1.call-done = f32[4,64,256]{2,1,0:T(8,128)} async-done(((f32[8,64,256]{2,1,0:T(8,128)}), f32[4,64,256]{2,1,0:T(8,128)}) %reduce-scatter.2.cloned.1.call-update) | async-done | bytes 262160 | tf_op jit(solution)/shard_map/reduce_scatter | solution.py:68
  (64 shorter events, 3.9 us)
Async XLA Ops:
  6.5 125.2 %reduce-scatter.2.cloned.1.call-start = ((), (), s32[]{:S(2)}) async-start(), calls=%async_computation.1 | async-start | bytes 786432 | tf_op jit(solution)/shard_map/reduce_scatter | solution.py:68
  6.5 60.4 %collective-permute-start.2 = (f32[16,64,512]{2,1,0:T(8,128)}, f32[16,64,512]{2,1,0:T(8,128)}, u32[]{:S(2)}, u32[]{:S(2)}) collective-permute-start(f32[16,64,512]{2,1,0:T(8,128)} %bitcast.87), channel_id=1, source_target_pairs={{0,24},{8,0},{16,8},{24,16},{1,25},{9,1},{17,9},{25,17},{2,26},{10... | collective-permute-start | bytes 6291464 | tf_op jit(solution)/shard_map/ppermute | solution.py:14
  8.9 57.3 %collective-permute-start.3 = (s32[16,8]{0,1:T(8,128)}, s32[16,8]{0,1:T(8,128)}, u32[]{:S(2)}, u32[]{:S(2)}) collective-permute-start(s32[16,8]{0,1:T(8,128)} %bitcast.93), channel_id=1, source_target_pairs={{0,24},{8,0},{16,8},{24,16},{1,25},{9,1},{17,9},{25,17},{2,26},{10... | collective-permute-start | bytes 1544 | tf_op jit(solution)/shard_map/ppermute | solution.py:14
  10.9 56.0 %collective-permute-start.1 = (s32[8,6]{1,0:T(8,128)}, s32[8,6]{1,0:T(8,128)}, u32[]{:S(2)}, u32[]{:S(2)}) collective-permute-start(s32[8,6]{1,0:T(8,128)} %bitcast.22), channel_id=1, source_target_pairs={{0,6},{2,0},{4,2},{6,4},{1,7},{3,1},{5,3},{7,5},{8,14},{10,8},{12,... | collective-permute-start | bytes 584 | tf_op jit(solution)/shard_map/ppermute | solution.py:14
  14.5 52.4 %collective-permute-start = (f32[8,64,384]{2,1,0:T(8,128)}, f32[8,64,384]{2,1,0:T(8,128)}, u32[]{:S(2)}, u32[]{:S(2)}) collective-permute-start(f32[8,64,384]{2,1,0:T(8,128)} %bitcast.89), channel_id=1, source_target_pairs={{0,6},{2,0},{4,2},{6,4},{1,7},{3,1},{5,3},{7,5},{8,14},{10,8},{12,... | collective-permute-start | bytes 2359304 | tf_op jit(solution)/shard_map/ppermute | solution.py:14
  29.1 6.3 %copy-start.4 = (pred[4,6]{1,0:T(4,128)(4,1)S(1)}, pred[4,6]{1,0:T(4,128)(4,1)}, u32[]{:S(2)}) copy-start(pred[4,6]{1,0:T(4,128)(4,1)} %get-tuple-element.227) | copy-start | bytes 76 | tf_op jit(solution)/shard_map/while
  35.6 5.4 %copy-start.2 = (f32[2,4,64,256]{3,2,1,0:T(8,128)S(1)}, f32[2,4,64,256]{3,2,1,0:T(8,128)}, u32[]{:S(2)}) copy-start(f32[2,4,64,256]{3,2,1,0:T(8,128)} %get-tuple-element.246) | copy-start | bytes 1572868 | tf_op jit(solution)/shard_map/while
  41.0 0.8 copy-start.3
  53.5 6.3 %copy-start.4 = (pred[4,6]{1,0:T(4,128)(4,1)S(1)}, pred[4,6]{1,0:T(4,128)(4,1)}, u32[]{:S(2)}) copy-start(pred[4,6]{1,0:T(4,128)(4,1)} %get-tuple-element.227) | copy-start | bytes 76 | tf_op jit(solution)/shard_map/while
  60.0 5.4 %copy-start.2 = (f32[2,4,64,256]{3,2,1,0:T(8,128)S(1)}, f32[2,4,64,256]{3,2,1,0:T(8,128)}, u32[]{:S(2)}) copy-start(f32[2,4,64,256]{3,2,1,0:T(8,128)} %get-tuple-element.246) | copy-start | bytes 1572868 | tf_op jit(solution)/shard_map/while
  65.4 0.8 copy-start.3
  79.5 6.3 %copy-start.5 = (pred[4,6]{1,0:T(4,128)(4,1)S(1)}, pred[4,6]{1,0:T(4,128)(4,1)}, u32[]{:S(2)}) copy-start(pred[4,6]{1,0:T(4,128)(4,1)} %get-tuple-element.236) | copy-start | bytes 76 | tf_op jit(solution)/shard_map/while
  86.0 5.4 %copy-start = (f32[2,4,64,256]{3,2,1,0:T(8,128)S(1)}, f32[2,4,64,256]{3,2,1,0:T(8,128)}, u32[]{:S(2)}) copy-start(f32[2,4,64,256]{3,2,1,0:T(8,128)} %get-tuple-element.270) | copy-start | bytes 1572868 | tf_op jit(solution)/shard_map/while
  91.3 0.9 copy-start.1
  103.9 6.3 %copy-start.5 = (pred[4,6]{1,0:T(4,128)(4,1)S(1)}, pred[4,6]{1,0:T(4,128)(4,1)}, u32[]{:S(2)}) copy-start(pred[4,6]{1,0:T(4,128)(4,1)} %get-tuple-element.236) | copy-start | bytes 76 | tf_op jit(solution)/shard_map/while
  110.4 5.4 %copy-start = (f32[2,4,64,256]{3,2,1,0:T(8,128)S(1)}, f32[2,4,64,256]{3,2,1,0:T(8,128)}, u32[]{:S(2)}) copy-start(f32[2,4,64,256]{3,2,1,0:T(8,128)} %get-tuple-element.270) | copy-start | bytes 1572868 | tf_op jit(solution)/shard_map/while
  115.8 0.9 copy-start.1
Sparse Core Ops, SparseCore 0:
  118.8 12.8 reduce-scatter.1
where the time goes:
time: 140 us; the launch traced here: 139 us
  local copies, waits for them, and re-layouts  54.5 us (39%)
  matrix products  43.3 us (31%)
  between operations  13.4 us (10%)
  waiting for transfers between devices  13 us (9%)
  starting transfers between devices  7.11 us (5%)
  other arithmetic  6.91 us (5%)
    dot_general x4, matrix products, block_term(): jnp.einsum('iawb,iwbv->iwav', blocks, gathered, precision=lax.Precision.H...  23.3 us
    reshape x4, local copies, waits for them, and re-layouts, block_term(): products = products.reshape(row_count, SLOTS_A, BLK, SLOTS_B, BLK)  22.4 us
    dot_general x4, matrix products, block_term(): jnp.einsum('iwvu,iwavc->iauc', matches, products, precision=lax.Precision...  20 us
    reduce_scatter x1, waiting for transfers between devices, per_device(): summed = lax.psum_scatter(running, 'layer', scatter_dimension=0, tiled=True)  13 us
    gather x4, local copies, waits for them, and re-layouts, block_term(): gathered = jnp.take(right_values, left_index, axis=0)  9.36 us
    ppermute x4, starting transfers between devices, shifted(): return lax.ppermute(x, axis, [(i, (i + by) % size) for i in range(size)])  7.1 us
    reshape x4, local copies, waits for them, and re-layouts, block_term(): blocks = left_values.reshape(row_count, BLK, SLOTS_A, BLK)  4.85 us
    and x4, other arithmetic, block_term(): gathered = jnp.take(right_values, left_index, axis=0)  4.79 us
  transfers between devices with their start and end apart: 5, of which 1 were waited for; matrix products, arithmetic and copies ran while one was open for 37% of the time, Pallas kernels for 0%

commit v1 on v0

v1 whole, which is shorter than its diff:
```python
import functools

import jax
import jax.numpy as jnp
from jax import lax
from jax.experimental import pallas as pl
from jax.experimental.pallas import tpu as pltpu
from jax.sharding import PartitionSpec as P

BLK = 64
SLOTS_A = 6
SLOTS_B = 8
KEEP = 4
LANES = 128
OWN_AT, SENT_AT, KEEP_AT, TARGET_AT = 0, 8, 16, 24


def kernel(
    sizes,
    a_hbm, b_hbm, ints_v, ints_s,
    out,
    own_a, far_a, b, rolled, targets, term0, term1, got0, got1,
    far_cols_v, far_keep_v, far_cols, far_keep,
    load_sem, a_send, a_recv, int_send, int_recv, int_load,
    send0, recv0, send1, recv1,
):
    grid_rows, grid_cols, layers = sizes
    rows = own_a.shape[0]
    krows = b.shape[0]
    share = rows // layers
    r, c, l = lax.axis_index("row"), lax.axis_index("col"), lax.axis_index("layer")
    up, down = lax.rem(r + 1, grid_rows), lax.rem(r + grid_rows - 1, grid_rows)
    right, left = lax.rem(c + 1, grid_cols), lax.rem(c + grid_cols - 1, grid_cols)

    barrier = pltpu.get_barrier_semaphore()
    partners = [(up, left, l), (down, right, l)]
    for other in range(layers):
        partners += [(up, c, other), (down, c, other)]
    for step in range(1, layers):
        partners.append((r, c, lax.rem(l + step, layers)))
    for partner in partners:
        pl.semaphore_signal(barrier, inc=1, device_id=partner, device_id_type=pl.DeviceIdType.MESH)

    own_image = lax.rem(r + c, grid_rows) // grid_cols
    sent_image = lax.rem(r + left + 1, grid_rows) // grid_cols
    load_b = pltpu.make_async_copy(b_hbm.at[:, 0, 0], b, load_sem.at[0])
    load_a = pltpu.make_async_copy(a_hbm.at[:, 0, 0, own_image], own_a, load_sem.at[1])
    load_b.start()
    load_a.start()
    pl.semaphore_wait(barrier, len(partners))

    def remote(src, dst, sent, received, target):
        return pltpu.make_async_remote_copy(
            src_ref=src, dst_ref=dst, send_sem=sent, recv_sem=received,
            device_id=target, device_id_type=pl.DeviceIdType.MESH,
        )

    move_cols = remote(ints_v, far_cols_v, int_send.at[0], int_recv.at[0], (up, left, l))
    move_keep = remote(ints_v, far_keep_v, int_send.at[1], int_recv.at[1], (up, c, l))
    move_cols.start()
    move_keep.start()

    def row_at(step):
        return lax.rem(step, layers) * share + step // layers

    def move_a(step):
        i = row_at(step)
        return remote(
            a_hbm.at[i, 0, 0, sent_image], far_a.at[i], a_send.at[i], a_recv.at[i], (up, left, l)
        )

    for step in range(rows):
        move_a(step).start()

    low = lax.broadcasted_iota(jnp.int32, (8, LANES), 1) < BLK
    load_b.wait()

    def prepare(k, carry):
        for pair in range(SLOTS_B // 2):
            cut = slice(pair * LANES, (pair + 1) * LANES)
            rolled[k, :, cut] = pltpu.roll(b[k, :, cut], BLK, 1)
            first = ints_s[k, TARGET_AT + 2 * pair]
            second = ints_s[k, TARGET_AT + 2 * pair + 1]
            targets[k, 2 * pair] = jnp.where(low, first, second)
            targets[k, 2 * pair + 1] = jnp.where(low, second, first)
        return carry

    lax.fori_loop(0, krows, prepare, 0)

    def row_term(a_row, i, cols, cols_at, keep):
        kept = [
            jnp.where(low, keep[i, KEEP_AT + 2 * half], keep[i, KEEP_AT + 2 * half + 1])
            for half in range(KEEP // 2)
        ]
        a_high = a_row.astype(jnp.bfloat16)
        a_low = (a_row - a_high.astype(jnp.float32)).astype(jnp.bfloat16)
        a_both = jnp.concatenate([a_high, a_low], axis=0)
        total = None
        for first in range(0, SLOTS_A, 2):
            picked = []
            for w in (first, first + 1):
                k = cols[i, cols_at + w]
                sums = [None] * (KEEP // 2)
                for slot in range(SLOTS_B):
                    cut = slice(slot // 2 * LANES, (slot // 2 + 1) * LANES)
                    source = b if slot % 2 == 0 else rolled
                    block = source[k, :, cut].reshape(BLK // 8, 8, LANES)
                    target = targets[k, slot]
                    for half in range(KEEP // 2):
                        mask = jnp.broadcast_to((target == kept[half])[None], block.shape)
                        part = jnp.where(mask, block, 0.0)
                        sums[half] = part if sums[half] is None else sums[half] + part
                picked.append(jnp.concatenate([s.reshape(BLK, LANES) for s in sums], axis=1))
            g = jnp.concatenate(picked, axis=0)
            g_high = g.astype(jnp.bfloat16)
            g_low = (g - g_high.astype(jnp.float32)).astype(jnp.bfloat16)
            cut = slice(first * BLK, (first + 2) * BLK)
            both = jnp.dot(a_both[:, cut], g_high, preferred_element_type=jnp.float32)
            part = both[:BLK] + both[BLK:] + jnp.dot(
                a_high[:, cut], g_low, preferred_element_type=jnp.float32
            )
            total = part if total is None else total + part
        return total

    def move_term0(i):
        return remote(
            term0.at[i], got0.at[l, lax.rem(i, share)], send0.at[i],
            recv0.at[l, lax.rem(i, share)], (r, c, i // share)
        )

    def move_term1(i):
        return remote(
            term1.at[i], got1.at[l, lax.rem(i, share)], send1.at[i],
            recv1.at[l, lax.rem(i, share)], (down, c, i // share)
        )

    load_a.wait()

    def other_rows(step, carry):
        i = lax.rem((l + 1) * share + step, rows)
        term0[i] = row_term(own_a[i], i, ints_s, OWN_AT, ints_s)
        move_term0(i).start()
        return carry

    def own_rows(step, carry):
        i = l * share + step
        term0[i] = row_term(own_a[i], i, ints_s, OWN_AT, ints_s)
        return carry

    lax.fori_loop(0, rows - share, other_rows, 0)
    lax.fori_loop(0, share, own_rows, 0)

    move_cols.wait_recv()
    move_keep.wait_recv()
    load_cols = pltpu.make_async_copy(far_cols_v, far_cols, int_load.at[0])
    load_keep = pltpu.make_async_copy(far_keep_v, far_keep, int_load.at[1])
    load_cols.start()
    load_keep.start()
    load_cols.wait()
    load_keep.wait()

    def far_rows(step, carry):
        i = row_at(step)
        move_a(step).wait_recv()
        term1[i] = row_term(far_a[i], i, far_cols, SENT_AT, far_keep)
        move_term1(i).start()
        return carry

    lax.fori_loop(0, rows, far_rows, 0)

    def final(j, carry):
        total = term0[l * share + j]
        for step in range(1, layers):
            other = lax.rem(l + step, layers)
            remote(term0.at[0], got0.at[other, j], send0.at[0], recv0.at[other, j], (r, c, other)).wait_recv()
            total = total + got0[other, j]
        for other in range(layers):
            remote(term1.at[0], got1.at[other, j], send1.at[0], recv1.at[other, j], (up, c, other)).wait_recv()
            total = total + got1[other, j]
        out[j, 0] = total
        return carry

    lax.fori_loop(0, share, final, 0)

    move_cols.wait_send()
    move_keep.wait_send()

    def sent_other(step, carry):
        move_term0(lax.rem((l + 1) * share + step, rows)).wait_send()
        return carry

    def sent_rows(i, carry):
        move_a(i).wait_send()
        move_term1(i).wait_send()
        return carry

    lax.fori_loop(0, rows - share, sent_other, 0)
    lax.fori_loop(0, rows, sent_rows, 0)


def per_device(a_values, a_columns, b_values, b_columns, keep_columns):
    sizes = tuple(lax.axis_size(name) for name in ("row", "col", "layer"))
    grid_rows, grid_cols, layers = sizes
    rows, krows = a_values.shape[0], b_values.shape[0]
    share = rows // layers
    r, c = lax.axis_index("row"), lax.axis_index("col")
    receiver = (c + grid_cols - 1) % grid_cols
    all_index = a_columns[:, 0, 0]
    own = lax.dynamic_index_in_dim(all_index, (r + c) % grid_rows // grid_cols, 1, keepdims=False)
    sent = lax.dynamic_index_in_dim(all_index, (r + receiver + 1) % grid_rows // grid_cols, 1, keepdims=False)

    def placed(x, at):
        return jnp.pad(x, ((0, krows - x.shape[0]), (at, LANES - at - x.shape[1])))

    ints = (
        placed(own, OWN_AT) + placed(sent, SENT_AT)
        + placed(keep_columns[:, 0], KEEP_AT) + placed(b_columns[:, 0, 0], TARGET_AT)
    )
    width = KEEP * BLK
    depth = SLOTS_A * BLK
    f32, i32 = jnp.float32, jnp.int32
    dma = pltpu.SemaphoreType.DMA
    return pl.pallas_call(
        functools.partial(kernel, sizes),
        out_shape=jax.ShapeDtypeStruct((share, 1, BLK, width), f32),
        in_specs=[
            pl.BlockSpec(memory_space=pl.ANY),
            pl.BlockSpec(memory_space=pl.ANY),
            pl.BlockSpec(memory_space=pltpu.VMEM),
            pl.BlockSpec(memory_space=pltpu.SMEM),
        ],
        out_specs=pl.BlockSpec(memory_space=pltpu.VMEM),
        scratch_shapes=[
            pltpu.VMEM((rows, BLK, depth), f32),
            pltpu.VMEM((rows, BLK, depth), f32),
            pltpu.VMEM((krows, BLK, SLOTS_B * BLK), f32),
            pltpu.VMEM((krows, BLK, SLOTS_B * BLK), f32),
            pltpu.VMEM((krows, SLOTS_B, 8, LANES), i32),
            pltpu.VMEM((rows, BLK, width), f32),
            pltpu.VMEM((rows, BLK, width), f32),
            pltpu.VMEM((layers, share, BLK, width), f32),
            pltpu.VMEM((layers, share, BLK, width), f32),
            pltpu.VMEM((krows, LANES), i32),
            pltpu.VMEM((krows, LANES), i32),
            pltpu.SMEM((krows, LANES), i32),
            pltpu.SMEM((krows, LANES), i32),
            dma((2,)), dma((rows,)), dma((rows,)), dma((2,)), dma((2,)), dma((2,)),
            dma((rows,)), dma((layers, share)), dma((rows,)), dma((layers, share)),
        ],
        compiler_params=pltpu.CompilerParams(
            collective_id=0, has_side_effects=True, vmem_limit_bytes=32 * 1024 * 1024
        ),
    )(a_values, b_values, ints, ints)


def solution(mesh):
    placed = (
        P("row", "col", "layer", None, None, None),
        P("row", "col", "layer", None, None),
        P("row", "col", "layer", None, None),
        P("row", "col", "layer", None),
        P("row", "col", None),
    )
    return jax.shard_map(
        per_device,
        mesh=mesh,
        in_specs=placed,
        out_specs=P(("row", "layer"), "col", None, None),
        check_vma=False,
    )
```

time: 140 us -> 33.5 us (0.24)
  the two profiles are of different devices: /device:TPU:0 before, /device:TPU:29 now
where the time goes in v1:
time: 33.5 us; the launch traced here: 33.2 us
  Pallas kernels  27.4 us (82%)
  local copies, waits for them, and re-layouts  5.7 us (17%)
    pallas_call x1, Pallas kernels, per_device(): pl.pallas_call(functools.partial(kernel, sizes), out_shape=jax.ShapeDtype...  27.4 us
    unnamed x6, local copies, waits for them, and re-layouts  4.19 us
    squeeze x1, local copies, waits for them, and re-layouts, per_device(): b_columns[:, 0, 0]  0.76 us
    squeeze x1, local copies, waits for them, and re-layouts, per_device(): keep_columns[:, 0]  0.76 us

profile of v1, /device:TPU:29, one launch (start us, length us, event | category | flops | bytes accessed | tf_op | source)
XLA Modules:
  0.0 33.2 jit_solution(8886698256494633720)
XLA Ops:
  0.0 0.8 %copy.6 = s32[8,1,1,1,6]{4,0,3,2,1:T(8,128)S(1)} copy(s32[8,1,1,1,6]{0,3,4,2,1:T(1,128)} %param.6) | data formatting | bytes 384 | tf_op args[1]
  0.8 0.8 %copy.7 = s32[8,4]{1,0:T(8,128)S(1)} copy(s32[8,4]{0,1:T(4,128)} %bitcast.5) | data formatting | bytes 256 | tf_op jit(solution)/shard_map/squeeze | solution.py:217
  1.5 0.8 %copy.8 = s32[16,8]{1,0:T(8,128)S(1)} copy(s32[16,8]{0,1:T(8,128)} %bitcast.4) | data formatting | bytes 1024 | tf_op jit(solution)/shard_map/squeeze | solution.py:217
  2.3 0.1 pad_add_fusion.ints_v.ints_s
  2.4 0.0 copy-start
  2.4 1.6 %copy-done = f32[16,1,1,64,512]{4,3,2,1,0:T(8,128)S(1)} copy-done((f32[16,1,1,64,512]{4,3,2,1,0:T(8,128)S(1)}, f32[16,1,1,64,512]{4,3,2,1,0:T(8,128)}, u32[]{:S(2)}) %copy-start) | copy-done | bytes 2097176
  3.9 0.0 copy-start.1
  3.9 1.1 %copy-done.1 = f32[8,1,1,1,64,384]{5,4,3,2,1,0:T(8,128)S(1)} copy-done((f32[8,1,1,1,64,384]{5,4,3,2,1,0:T(8,128)S(1)}, f32[8,1,1,1,64,384]{5,4,3,2,1,0:T(8,128)}, u32[]{:S(2)}) %copy-start.1) | copy-done | bytes 786456
  5.1 27.4 %shard_map.55 = f32[4,1,64,256]{3,2,1,0:T(8,128)S(1)} custom-call(f32[8,1,1,1,64,384]{5,4,3,2,1,0:T(8,128)S(1)} %copy-done.1, f32[16,1,1,64,512]{4,3,2,1,0:T(8,128)S(1)} %copy-done, s32[16,128]{1,0:T(8,128)S(1)} %pad_add_fusion.ints_v.ints_s, s32[16,128]{1,0:T(8,128)S(1)} %pad_add_fusion.ints_v.ints_s), custom_call_target="tpu_custom_call" | custom-call | tf_op jit(solution)/shard_map/pallas_call | solution.py:223
  32.5 0.7 %copy.10 = f32[4,1,64,256]{3,2,1,0:T(8,128)} copy(f32[4,1,64,256]{3,2,1,0:T(8,128)S(1)} %shard_map.55) | data formatting | bytes 524288
Async XLA Ops:
  2.4 1.6 %copy-start = (f32[16,1,1,64,512]{4,3,2,1,0:T(8,128)S(1)}, f32[16,1,1,64,512]{4,3,2,1,0:T(8,128)}, u32[]{:S(2)}) copy-start(f32[16,1,1,64,512]{4,3,2,1,0:T(8,128)} %b_hbm.1) | copy-start | bytes 6291460
  3.9 1.1 %copy-start.1 = (f32[8,1,1,1,64,384]{5,4,3,2,1,0:T(8,128)S(1)}, f32[8,1,1,1,64,384]{5,4,3,2,1,0:T(8,128)}, u32[]{:S(2)}) copy-start(f32[8,1,1,1,64,384]{5,4,3,2,1,0:T(8,128)} %a_hbm.1) | copy-start | bytes 2359300

commit v2 on v1

v2 whole, which is shorter than its diff:
```python
import functools

import jax
import jax.numpy as jnp
from jax import lax
from jax.experimental import pallas as pl
from jax.experimental.pallas import tpu as pltpu
from jax.sharding import PartitionSpec as P

BLK = 64
SLOTS_A = 6
SLOTS_B = 8
KEEP = 4
LANES = 128


def kernel(
    sizes,
    a_hbm, b_hbm, cols_hbm, keep_hbm, targets_hbm,
    out,
    own_a, far_a, b, rolled, targets, g_high, g_low, term0, term1, got0, got1,
    own_cols, own_keep, own_targets, far_cols_v, far_keep_v, far_cols, far_keep,
    load_sem, a_send, a_recv, int_send, int_recv, int_load,
    send0, recv0, send1, recv1,
):
    grid_rows, grid_cols, layers = sizes
    rows = own_a.shape[0]
    krows = b.shape[0]
    share = rows // layers
    r, c, l = lax.axis_index("row"), lax.axis_index("col"), lax.axis_index("layer")
    up, down = lax.rem(r + 1, grid_rows), lax.rem(r + grid_rows - 1, grid_rows)
    right, left = lax.rem(c + 1, grid_cols), lax.rem(c + grid_cols - 1, grid_cols)

    barrier = pltpu.get_barrier_semaphore()
    senders = [(down, right, l), (down, c, l)]
    senders += [(up, c, other) for other in range(layers)]
    senders += [(r, c, lax.rem(l + step, layers)) for step in range(1, layers)]
    for partner in senders:
        pl.semaphore_signal(barrier, inc=1, device_id=partner, device_id_type=pl.DeviceIdType.MESH)

    own_image = lax.rem(r + c, grid_rows) // grid_cols
    sent_image = lax.rem(r + left + 1, grid_rows) // grid_cols
    load_b = pltpu.make_async_copy(b_hbm.at[:, 0, 0], b, load_sem.at[0])
    load_a = pltpu.make_async_copy(a_hbm.at[:, 0, 0, own_image], own_a, load_sem.at[1])
    load_ints = [
        pltpu.make_async_copy(src, dst, load_sem.at[2 + at])
        for at, (src, dst) in enumerate(
            [(cols_hbm, own_cols), (keep_hbm, own_keep), (targets_hbm, own_targets)]
        )
    ]
    load_b.start()
    load_a.start()
    for load in load_ints:
        load.start()
    pl.semaphore_wait(barrier, len(senders))

    def remote(src, dst, sent, received, target):
        return pltpu.make_async_remote_copy(
            src_ref=src, dst_ref=dst, send_sem=sent, recv_sem=received,
            device_id=target, device_id_type=pl.DeviceIdType.MESH,
        )

    move_cols = remote(cols_hbm, far_cols_v, int_send.at[0], int_recv.at[0], (up, left, l))
    move_keep = remote(keep_hbm, far_keep_v, int_send.at[1], int_recv.at[1], (up, c, l))
    move_cols.start()
    move_keep.start()

    def row_at(step):
        return lax.rem(step, layers) * share + step // layers

    def move_a(step):
        i = row_at(step)
        return remote(
            a_hbm.at[i, 0, 0, sent_image], far_a.at[i], a_send.at[i], a_recv.at[i], (up, left, l)
        )

    for step in range(rows):
        move_a(step).start()

    low = lax.broadcasted_iota(jnp.int32, (8, LANES), 1) < BLK
    load_b.wait()
    for load in load_ints:
        load.wait()

    def prepare(k, carry):
        for pair in range(SLOTS_B // 2):
            cut = slice(pair * LANES, (pair + 1) * LANES)
            rolled[k, :, cut] = pltpu.roll(b[k, :, cut], BLK, 1)
            first = own_targets[2 * pair, k]
            second = own_targets[2 * pair + 1, k]
            targets[k, 2 * pair] = jnp.where(low, first, second)
            targets[k, 2 * pair + 1] = jnp.where(low, second, first)
        return carry

    lax.fori_loop(0, krows, prepare, 0)

    def gather(i, cols, keep):
        kept = [
            jnp.where(low, keep[2 * half, i], keep[2 * half + 1, i])
            for half in range(KEEP // 2)
        ]
        for w in range(SLOTS_A):
            k = cols[w, own_image, i]
            sums = [None] * (KEEP // 2)
            for slot in range(SLOTS_B):
                cut = slice(slot // 2 * LANES, (slot // 2 + 1) * LANES)
                source = b if slot % 2 == 0 else rolled
                block = source[k, :, cut].reshape(BLK // 8, 8, LANES)
                target = targets[k, slot]
                for half in range(KEEP // 2):
                    mask = jnp.broadcast_to((target == kept[half])[None], block.shape)
                    part = jnp.where(mask, block, 0.0)
                    sums[half] = part if sums[half] is None else sums[half] + part
            g = jnp.concatenate([s.reshape(BLK, LANES) for s in sums], axis=1)
            high = g.astype(jnp.bfloat16)
            g_high[i, w * BLK:(w + 1) * BLK, :] = high
            g_low[i, w * BLK:(w + 1) * BLK, :] = (g - high.astype(jnp.float32)).astype(jnp.bfloat16)

    def multiply(a_row, i):
        a_high = a_row.astype(jnp.bfloat16)
        a_low = (a_row - a_high.astype(jnp.float32)).astype(jnp.bfloat16)
        both = jnp.dot(
            jnp.concatenate([a_high, a_low], axis=0), g_high[i], preferred_element_type=jnp.float32
        )
        return both[:BLK] + both[BLK:] + jnp.dot(
            a_high, g_low[i], preferred_element_type=jnp.float32
        )

    def move_term0(i):
        return remote(
            term0.at[i], got0.at[l, lax.rem(i, share)], send0.at[i],
            recv0.at[l, lax.rem(i, share)], (r, c, i // share)
        )

    def move_term1(i):
        return remote(
            term1.at[i], got1.at[l, lax.rem(i, share)], send1.at[i],
            recv1.at[l, lax.rem(i, share)], (down, c, i // share)
        )

    load_a.wait()

    def other_rows(step, carry):
        i = lax.rem((l + 1) * share + step, rows)
        gather(i, own_cols, own_keep)
        term0[i] = multiply(own_a[i], i)
        move_term0(i).start()
        return carry

    def own_rows(step, carry):
        i = l * share + step
        gather(i, own_cols, own_keep)
        term0[i] = multiply(own_a[i], i)
        return carry

    lax.fori_loop(0, rows - share, other_rows, 0)
    lax.fori_loop(0, share, own_rows, 0)

    move_cols.wait_recv()
    move_keep.wait_recv()
    load_cols = pltpu.make_async_copy(far_cols_v, far_cols, int_load.at[0])
    load_keep = pltpu.make_async_copy(far_keep_v, far_keep, int_load.at[1])
    load_cols.start()
    load_keep.start()
    load_cols.wait()
    load_keep.wait()

    def far_gather(i, carry):
        gather(i, far_cols, far_keep)
        return carry

    lax.fori_loop(0, rows, far_gather, 0)

    def far_rows(step, carry):
        i = row_at(step)
        move_a(step).wait_recv()
        term1[i] = multiply(far_a[i], i)
        move_term1(i).start()
        return carry

    lax.fori_loop(0, rows, far_rows, 0)

    def final(j, carry):
        total = term0[l * share + j]
        for step in range(1, layers):
            other = lax.rem(l + step, layers)
            remote(term0.at[0], got0.at[other, j], send0.at[0], recv0.at[other, j], (r, c, other)).wait_recv()
            total = total + got0[other, j]
        for other in range(layers):
            remote(term1.at[0], got1.at[other, j], send1.at[0], recv1.at[other, j], (up, c, other)).wait_recv()
            total = total + got1[other, j]
        out[j, 0] = total
        return carry

    lax.fori_loop(0, share, final, 0)

    move_cols.wait_send()
    move_keep.wait_send()

    def sent_other(step, carry):
        move_term0(lax.rem((l + 1) * share + step, rows)).wait_send()
        return carry

    def sent_rows(i, carry):
        move_a(i).wait_send()
        move_term1(i).wait_send()
        return carry

    lax.fori_loop(0, rows - share, sent_other, 0)
    lax.fori_loop(0, rows, sent_rows, 0)


def per_device(a_values, a_columns, b_values, b_columns, keep_columns):
    sizes = tuple(lax.axis_size(name) for name in ("row", "col", "layer"))
    layers = sizes[2]
    rows, krows = a_values.shape[0], b_values.shape[0]
    share = rows // layers
    cols = jnp.transpose(a_columns[:, 0, 0], (2, 1, 0))
    keep = jnp.transpose(keep_columns[:, 0])
    targets = jnp.transpose(b_columns[:, 0, 0])
    width = KEEP * BLK
    depth = SLOTS_A * BLK
    f32, i32 = jnp.float32, jnp.int32
    dma = pltpu.SemaphoreType.DMA
    return pl.pallas_call(
        functools.partial(kernel, sizes),
        out_shape=jax.ShapeDtypeStruct((share, 1, BLK, width), f32),
        in_specs=[
            pl.BlockSpec(memory_space=pltpu.HBM),
            pl.BlockSpec(memory_space=pltpu.HBM),
            pl.BlockSpec(memory_space=pltpu.HBM),
            pl.BlockSpec(memory_space=pltpu.HBM),
            pl.BlockSpec(memory_space=pltpu.HBM),
        ],
        out_specs=pl.BlockSpec(memory_space=pltpu.VMEM),
        scratch_shapes=[
            pltpu.VMEM((rows, BLK, depth), f32),
            pltpu.VMEM((rows, BLK, depth), f32),
            pltpu.VMEM((krows, BLK, SLOTS_B * BLK), f32),
            pltpu.VMEM((krows, BLK, SLOTS_B * BLK), f32),
            pltpu.VMEM((krows, SLOTS_B, 8, LANES), i32),
            pltpu.VMEM((rows, depth, width), jnp.bfloat16),
            pltpu.VMEM((rows, depth, width), jnp.bfloat16),
            pltpu.VMEM((rows, BLK, width), f32),
            pltpu.VMEM((rows, BLK, width), f32),
            pltpu.VMEM((layers, share, BLK, width), f32),
            pltpu.VMEM((layers, share, BLK, width), f32),
            pltpu.SMEM(cols.shape, i32),
            pltpu.SMEM(keep.shape, i32),
            pltpu.SMEM(targets.shape, i32),
            pltpu.VMEM(cols.shape, i32),
            pltpu.VMEM(keep.shape, i32),
            pltpu.SMEM(cols.shape, i32),
            pltpu.SMEM(keep.shape, i32),
            dma((5,)), dma((rows,)), dma((rows,)), dma((2,)), dma((2,)), dma((2,)),
            dma((rows,)), dma((layers, share)), dma((rows,)), dma((layers, share)),
        ],
        compiler_params=pltpu.CompilerParams(
            collective_id=0, has_side_effects=True, vmem_limit_bytes=60 * 1024 * 1024
        ),
    )(a_values, b_values, cols, keep, targets)


def solution(mesh):
    placed = (
        P("row", "col", "layer", None, None, None),
        P("row", "col", "layer", None, None),
        P("row", "col", "layer", None, None),
        P("row", "col", "layer", None),
        P("row", "col", None),
    )
    return jax.shard_map(
        per_device,
        mesh=mesh,
        in_specs=placed,
        out_specs=P(("row", "layer"), "col", None, None),
        check_vma=False,
    )
```

time: 33.5 us -> 29.1 us (0.87)
  local copies, waits for them, and re-layouts: 5.7 us -> 1.67 us
    unnamed x6 -> x1, local copies, waits for them, and re-layouts: 4.19 us -> 1.67 us
    squeeze x2 -> x0, local copies, waits for them, and re-layouts: 1.51 us -> none  [the longest x1 0.76 us: per_device(): b_columns[:, 0, 0]]
where the time goes in v2:
time: 29.1 us; the launch traced here: 29 us
  Pallas kernels  27.3 us (94%)
  local copies, waits for them, and re-layouts  1.67 us (6%)
    pallas_call x1, Pallas kernels, per_device(): pl.pallas_call(functools.partial(kernel, sizes), out_shape=jax.ShapeDtype...  27.3 us
    unnamed x1, local copies, waits for them, and re-layouts  1.67 us

profile of v2, /device:TPU:29, one launch (start us, length us, event | category | flops | bytes accessed | tf_op | source)
XLA Modules:
  0.0 29.0 jit_solution(2084903948141395941)
XLA Ops:
  0.0 27.3 %shard_map.55 = f32[4,1,64,256]{3,2,1,0:T(8,128)} custom-call(f32[8,1,1,1,64,384]{5,4,3,2,1,0:T(8,128)} %a_hbm.1, f32[16,1,1,64,512]{4,3,2,1,0:T(8,128)} %b_hbm.1, s32[6,1,8]{2,1,0:T(1,128)} %bitcast.10, s32[4,8]{1,0:T(4,128)} %bitcast.11, s32[8,16]{1,0:T(8,128)} %bitcast.9), custom_call_target="tpu_custom_call" | custom-call | tf_op jit(solution)/shard_map/pallas_call | solution.py:225
  27.3 1.7 %copy.7 = f32[4,1,64,256]{3,2,1,0:T(8,128)} copy(f32[4,1,64,256]{3,2,1,0:T(8,128)} %shard_map.55) | data formatting | bytes 524288

commit v3 on v2

--- a/solution.py
+++ b/solution.py
@@ -256,9 +256,9 @@
             dma((rows,)), dma((layers, share)), dma((rows,)), dma((layers, share)),
         ],
         compiler_params=pltpu.CompilerParams(
-            collective_id=0, has_side_effects=True, vmem_limit_bytes=60 * 1024 * 1024
+            collective_id=0, has_side_effects=True, vmem_limit_bytes=32 * 1024 * 1024
         ),
-    )(a_values, b_values, cols, keep, targets)
+    )(*(pltpu.with_memory_space_constraint(x, pltpu.HBM) for x in (a_values, b_values, cols, keep, targets)))
 
 
 def solution(mesh):

time: 29.1 us -> 27.5 us (0.945)
  local copies, waits for them, and re-layouts: 1.67 us -> 0.71 us
  Pallas kernels: 27.3 us -> 26.6 us
    unnamed x1, local copies, waits for them, and re-layouts: 1.67 us -> 0.71 us
    pallas_call x1, Pallas kernels: 27.3 us -> 26.6 us  [per_device(): pl.pallas_call(functools.partial(kernel, sizes), out_shape=jax.ShapeDtype...]
where the time goes in v3:
time: 27.5 us; the launch traced here: 27.3 us
  Pallas kernels  26.6 us (97%)
  local copies, waits for them, and re-layouts  0.71 us (3%)
    pallas_call x1, Pallas kernels, per_device(): pl.pallas_call(functools.partial(kernel, sizes), out_shape=jax.ShapeDtype...  26.6 us
    unnamed x1, local copies, waits for them, and re-layouts  0.71 us

profile of v3, /device:TPU:29, one launch (start us, length us, event | category | flops | bytes accessed | tf_op | source)
XLA Modules:
  0.0 27.3 jit_solution(16072484376872270850)
XLA Ops:
  0.0 26.6 %shard_map.55 = f32[4,1,64,256]{3,2,1,0:T(8,128)S(1)} custom-call(f32[8,1,1,1,64,384]{5,4,3,2,1,0:T(8,128)} %a_hbm.1, f32[16,1,1,64,512]{4,3,2,1,0:T(8,128)} %b_hbm.1, s32[6,1,8]{2,1,0:T(1,128)} %bitcast.10, s32[4,8]{1,0:T(4,128)} %bitcast.11, s32[8,16]{1,0:T(8,128)} %bitcast.9), custom_call_target="tpu_custom_call" | custom-call | tf_op jit(solution)/shard_map/pallas_call | solution.py:225
  26.6 0.7 %copy.7 = f32[4,1,64,256]{3,2,1,0:T(8,128)} copy(f32[4,1,64,256]{3,2,1,0:T(8,128)S(1)} %shard_map.55) | data formatting | bytes 524288

commit v4 on v3

--- a/solution.py
+++ b/solution.py
@@ -48,8 +48,6 @@
             [(cols_hbm, own_cols), (keep_hbm, own_keep), (targets_hbm, own_targets)]
         )
     ]
-    load_b.start()
-    load_a.start()
     for load in load_ints:
         load.start()
     pl.semaphore_wait(barrier, len(senders))
@@ -76,6 +74,8 @@
 
     for step in range(rows):
         move_a(step).start()
+    load_b.start()
+    load_a.start()
 
     low = lax.broadcasted_iota(jnp.int32, (8, LANES), 1) < BLK
     load_b.wait()
@@ -171,6 +171,17 @@
 
     lax.fori_loop(0, rows, far_gather, 0)
 
+    def early(j, carry):
+        total = term0[l * share + j]
+        for step in range(1, layers):
+            other = lax.rem(l + step, layers)
+            remote(term0.at[0], got0.at[other, j], send0.at[0], recv0.at[other, j], (r, c, other)).wait_recv()
+            total = total + got0[other, j]
+        out[j, 0] = total
+        return carry
+
+    lax.fori_loop(0, share, early, 0)
+
     def far_rows(step, carry):
         i = row_at(step)
         move_a(step).wait_recv()
@@ -181,11 +192,7 @@
     lax.fori_loop(0, rows, far_rows, 0)
 
     def final(j, carry):
-        total = term0[l * share + j]
-        for step in range(1, layers):
-            other = lax.rem(l + step, layers)
-            remote(term0.at[0], got0.at[other, j], send0.at[0], recv0.at[other, j], (r, c, other)).wait_recv()
-            total = total + got0[other, j]
+        total = out[j, 0]
         for other in range(layers):
             remote(term1.at[0], got1.at[other, j], send1.at[0], recv1.at[other, j], (up, c, other)).wait_recv()
             total = total + got1[other, j]

time: 27.5 us -> 27.4 us (level)
  no operation moved by 1% of the time
where the time goes in v4:
time: 27.4 us; the launch traced here: 27.3 us
  Pallas kernels  26.6 us (97%)
  local copies, waits for them, and re-layouts  0.71 us (3%)
    pallas_call x1, Pallas kernels, per_device(): pl.pallas_call(functools.partial(kernel, sizes), out_shape=jax.ShapeDtype...  26.6 us
    unnamed x1, local copies, waits for them, and re-layouts  0.71 us

profile of v4, /device:TPU:29, one launch (start us, length us, event | category | flops | bytes accessed | tf_op | source)
XLA Modules:
  0.0 27.3 jit_solution(1962156086640657976)
XLA Ops:
  0.0 26.6 %shard_map.55 = f32[4,1,64,256]{3,2,1,0:T(8,128)S(1)} custom-call(f32[8,1,1,1,64,384]{5,4,3,2,1,0:T(8,128)} %a_hbm.1, f32[16,1,1,64,512]{4,3,2,1,0:T(8,128)} %b_hbm.1, s32[6,1,8]{2,1,0:T(1,128)} %bitcast.10, s32[4,8]{1,0:T(4,128)} %bitcast.11, s32[8,16]{1,0:T(8,128)} %bitcast.9), custom_call_target="tpu_custom_call" | custom-call | tf_op jit(solution)/shard_map/pallas_call | solution.py:232
  26.6 0.7 %copy.7 = f32[4,1,64,256]{3,2,1,0:T(8,128)} copy(f32[4,1,64,256]{3,2,1,0:T(8,128)S(1)} %shard_map.55) | data formatting | bytes 524288
